TPU v7x, 32 devices: a whole 2x2x4 slice. The times are simulated.
32 devices in a mesh: segment: 2 (over y), lon: 4 (over x, core), lat: 4 (over z).
Axes of the slice: x: 2, y: 2, z: 4, core: 2. Of those that a mesh axis runs over, the one named last changes fastest.
Arguments:
- latents: bfloat16 [2, 24, 48, 1024], P(None, 'lat', 'lon'), may hold values from -48 to 48
- land_mask: int32 [24, 48], P('lat', 'lon'), may hold values 0 or 1
- land_embed: bfloat16 [1024], replicated, may hold values from -6 to 6
- qkv_weight: bfloat16 [2, 1024, 3072], P('segment'), may hold values from -0.25625 to 0.25625
- out_weight: bfloat16 [2, 1024, 1024], P('segment'), may hold values from -0.5625 to 0.5625
- norm_gain: float32 [2, 1024], replicated, may hold values from 0.5 to 1.5
- offsets: int32 [2, 2], replicated, may hold values from 0 to 11, as said below
Outputs:
- sections: bfloat16 [2, 2, 24, 48, 1024], P('segment', None, 'lat', 'lon')
Inputs may be any that keep to these rules, and one draw needn't show every extreme that they name: offsets[s, 0] lies in 0 to 5 and offsets[s, 1] in 0 to 11; one of the two sections has offsets[s, 0] = 5 and offsets[s, 1] = 11.
All inputs are finite; a program needn't handle non-finite values. No bound on the sum of `land_mask` on one device may be relied on, other than what follows from the above.
Results may differ from a plain program's by a relative error of at most 0.015.
Values may be sent and summed in bfloat16 or wider, within the bound.
A program may use at most 64 MiB of HBM per device.

v0:
```python
import functools
import math

import jax
import jax.numpy as jnp
from jax import lax
from jax.experimental import pallas as pl
from jax.experimental.pallas import tpu as pltpu
from jax.sharding import PartitionSpec as P

HEADS = 16
WLAT = 6
WLON = 12
HALF_LAT = WLAT // 2
HALF_LON = WLON // 2
STEPS = 4
PAIR = 128
NT = (((1,), (1,)), ((), ()))


def based(offset, window):
    return jnp.where(offset >= window // 2, offset - window, offset)


def cell_codes(base, offset, shape, axis, total_rows):
    cell = lax.broadcasted_iota(jnp.int32, shape, axis)
    line = jnp.zeros(shape, jnp.int32)
    for start in range(WLON, shape[axis], WLON):
        line += (cell >= start).astype(jnp.int32)
    block = jnp.zeros(shape, jnp.int32)
    for start in range(WLAT, shape[axis] // WLON, WLAT):
        block += (line >= start).astype(jnp.int32)
    held = base + line - WLAT * block
    held = jnp.where(held < 0, held + total_rows, held)
    held = jnp.where(held >= total_rows, held - total_rows, held)
    return 2 * block + (held < offset).astype(jnp.int32)


def attend_kernel(section, offsets_ref, x_ref, wq_ref, wk_ref, wv_ref, wo_ref, gain_ref, out_ref, total, *, head_size, total_rows):
    step = pl.program_id(0)
    x = x_ref[...]
    q = jnp.dot(x, wq_ref[...], preferred_element_type=jnp.float32).astype(jnp.bfloat16)
    k = jnp.dot(x, wk_ref[...], preferred_element_type=jnp.float32).astype(jnp.bfloat16)
    v = jnp.dot(x, wv_ref[...], preferred_element_type=jnp.float32).astype(jnp.bfloat16)
    cells = x.shape[0]
    offset = offsets_ref[section, 0]
    base = lax.axis_index("lat") * WLAT + based(offset, WLAT)
    allowed = cell_codes(base, offset, (cells, 1), 0, total_rows) == cell_codes(base, offset, (1, cells), 1, total_rows)
    scale = 1.0 / math.sqrt(head_size)
    first_half = lax.broadcasted_iota(jnp.int32, (x.shape[0], PAIR), 1) < head_size
    parts = []
    for pair in range(q.shape[1] // PAIR):
        columns = slice(pair * PAIR, (pair + 1) * PAIR)
        q2, k2, v2 = q[:, columns], k[:, columns], v[:, columns]
        weighted = []
        for keep in (first_half, ~first_half):
            qh = jnp.where(keep, q2, jnp.zeros_like(q2))
            scores = lax.dot_general(qh, k2, NT, preferred_element_type=jnp.float32) * scale
            scores = jnp.where(allowed, scores, -1e30)
            weights = jnp.exp(scores - jnp.max(scores, axis=-1, keepdims=True))
            inverse = 1.0 / jnp.sum(weights, axis=-1, keepdims=True)
            probs = (weights * inverse).astype(jnp.bfloat16)
            weighted.append(jnp.dot(probs, v2, preferred_element_type=jnp.float32))
        parts.append(jnp.where(first_half, weighted[0], weighted[1]).astype(jnp.bfloat16))
    attended = jnp.concatenate(parts, axis=1)
    projected = jnp.dot(attended, wo_ref[...], preferred_element_type=jnp.float32)

    @pl.when(step == 0)
    def _():
        total[...] = projected

    @pl.when(step > 0)
    def _():
        total[...] += projected

    @pl.when(step == STEPS - 1)
    def _():
        whole = total[...]
        gain = jnp.where(lax.axis_index("segment") == 0, gain_ref[0:1, :], gain_ref[1:2, :])
        centered = whole - jnp.mean(whole, axis=-1, keepdims=True)
        variance = jnp.mean(centered * centered, axis=-1, keepdims=True)
        branch = centered * lax.rsqrt(variance + 1e-05) * gain
        out_ref[...] = (x.astype(jnp.float32) + branch).astype(jnp.bfloat16)


def attend(field, section, offsets, wqkv, wout, gain):
    width = field.shape[-1]
    flat = field.reshape(-1, width)
    cells = flat.shape[0]
    slab = width // STEPS
    head_size = width // HEADS
    full = lambda shape: pl.BlockSpec(shape, lambda p: (0, 0))
    return pl.pallas_call(
        functools.partial(
            attend_kernel, section, head_size=head_size, total_rows=WLAT * lax.axis_size("lat")
        ),
        grid=(STEPS,),
        out_shape=jax.ShapeDtypeStruct((cells, width), jnp.bfloat16),
        in_specs=[
            pl.BlockSpec(memory_space=pltpu.SMEM),
            full((cells, width)),
            pl.BlockSpec((width, slab), lambda p: (0, p)),
            pl.BlockSpec((width, slab), lambda p: (0, p + STEPS)),
            pl.BlockSpec((width, slab), lambda p: (0, p + 2 * STEPS)),
            pl.BlockSpec((slab, width), lambda p: (p, 0)),
            full(gain.shape),
        ],
        out_specs=full((cells, width)),
        scratch_shapes=[pltpu.VMEM((cells, width), jnp.float32)],
        compiler_params=pltpu.CompilerParams(vmem_limit_bytes=56 * 1024 * 1024),
        cost_estimate=pl.CostEstimate(
            flops=8 * cells * width * width, bytes_accessed=8 * width * width, transcendentals=HEADS * cells * cells
        ),
    )(offsets, flat, wqkv, wqkv, wqkv, wout, gain)


def exchange_kernel(lat_steps, lon_steps, below_in, corner_in, beside_in, below, corner, beside, send_sem, recv_sem):
    segment, lon, lat = (lax.axis_index(axis) for axis in ("segment", "lon", "lat"))
    lons, lats = lax.axis_size("lon"), lax.axis_size("lat")
    pick = lambda steps: steps[0] + segment * (steps[1] - steps[0])
    lat_step, lon_step = pick(lat_steps), pick(lon_steps)
    place = lambda a, b: (segment, lax.rem(lon + b + lons, lons), lax.rem(lat + a + lats, lats))
    ways = ((lat_step, lon_step), (lat_step, 0), (0, lon_step))
    barrier = pltpu.get_barrier_semaphore()
    for a, b in ways:
        pl.semaphore_signal(barrier, inc=1, device_id=place(a, b), device_id_type=pl.DeviceIdType.MESH)
    pl.semaphore_wait(barrier, 3)
    copies = []
    for index, ((a, b), source, target) in enumerate(
        zip(ways, (corner_in, below_in, beside_in), (corner, below, beside))
    ):
        copy = pltpu.make_async_remote_copy(
            src_ref=source,
            dst_ref=target,
            send_sem=send_sem.at[index],
            recv_sem=recv_sem.at[index],
            device_id=place(-a, -b),
            device_id_type=pl.DeviceIdType.MESH,
        )
        copy.start()
        copies.append(copy)
    for copy in copies:
        copy.wait()


def exchanged(lat_steps, lon_steps, pieces):
    width = pieces[0].shape[-1]
    flats = []
    for piece in pieces:
        flat = piece.reshape(-1, width)
        flats.append(jnp.pad(flat, ((0, -flat.shape[0] % 16), (0, 0))))
    signs = [(1, 1), (1, -1), (-1, 1), (-1, -1)]
    in_vmem = pl.BlockSpec(memory_space=pltpu.VMEM)
    results = pl.pallas_call(
        functools.partial(exchange_kernel, lat_steps, lon_steps),
        out_shape=[jax.ShapeDtypeStruct(flat.shape, flat.dtype) for flat in flats],
        in_specs=[in_vmem] * 3,
        out_specs=[in_vmem] * 3,
        scratch_shapes=[pltpu.SemaphoreType.DMA((3,)), pltpu.SemaphoreType.DMA((3,))],
        compiler_params=pltpu.CompilerParams(
            collective_id=4 * signs.index(lat_steps) + signs.index(lon_steps),
            has_side_effects=True,
            vmem_limit_bytes=8 * 1024 * 1024,
        ),
    )(*flats)
    return [out[: math.prod(piece.shape[:-1])].reshape(piece.shape) for out, piece in zip(results, pieces)]


def by_segment(make, steps):
    if steps[0] == steps[1]:
        return make(steps[0])
    return jnp.where(lax.axis_index("segment") == 0, make(steps[0]), make(steps[1]))


def neighbours(lat_steps, lon_steps, field):
    rows = lambda step: field[:, :HALF_LAT] if step > 0 else field[:, WLAT - HALF_LAT:]
    columns = lambda part: lambda step: part[:, :, :HALF_LON] if step > 0 else part[:, :, WLON - HALF_LON:]
    row_piece = by_segment(rows, lat_steps)
    corner_piece = by_segment(columns(row_piece), lon_steps)
    column_piece = by_segment(columns(field), lon_steps)
    return exchanged(lat_steps, lon_steps, (row_piece, corner_piece, column_piece))


def assembled(field, below, corner, beside, lat_shift, lon_shift):
    near = jnp.concatenate([beside, field, beside], axis=2)
    near = lax.dynamic_slice_in_dim(near, HALF_LON + lon_shift, field.shape[2], 2)
    far = jnp.concatenate([corner, below, corner], axis=2)
    far = lax.dynamic_slice_in_dim(far, HALF_LON + lon_shift, field.shape[2], 2)
    tall = jnp.concatenate([far, near, far], axis=1)
    return lax.dynamic_slice_in_dim(tall, HALF_LAT + lat_shift, field.shape[1], 1)


def sign_of(lat_shift, lon_shift):
    return 2 * (lat_shift < 0).astype(jnp.int32) + (lon_shift < 0).astype(jnp.int32)


def shift(field, lat_shift, lon_shift):
    ways = [functools.partial(neighbours, (a, a), (b, b)) for a in (1, -1) for b in (1, -1)]
    pieces = lax.switch(sign_of(lat_shift, lon_shift), ways, field)
    return assembled(field, *pieces, lat_shift, lon_shift)


def shift_each(field, lat_shifts, lon_shifts):
    signs = [sign_of(*pair) for pair in zip(lat_shifts, lon_shifts)]
    choice = jnp.where(signs[1] > 0, 4 + signs[1], signs[0])
    ways = []
    for segment in (0, 1):
        for a in (1, -1):
            for b in (1, -1):
                lat_steps = (a, 1) if segment == 0 else (1, a)
                lon_steps = (b, 1) if segment == 0 else (1, b)
                ways.append(functools.partial(neighbours, lat_steps, lon_steps))
    pieces = lax.switch(choice, ways, field)
    first = lax.axis_index("segment") == 0
    return assembled(field, *pieces, jnp.where(first, *lat_shifts), jnp.where(first, *lon_shifts))


def body(latents, land_mask, land_embed, qkv_weight, out_weight, norm_gain, offsets):
    segment_index = lax.axis_index("segment")
    assert latents.shape[1:3] == (WLAT, WLON)
    embedded = latents.astype(jnp.float32) + land_embed.astype(jnp.float32)
    seeded = jnp.where(land_mask[None, :, :, None] > 0, embedded, latents.astype(jnp.float32)).astype(jnp.bfloat16)
    wqkv = qkv_weight[0]
    wout = out_weight[0]
    lat_base, lon_base = [], []
    for s in (0, 1):
        lat_base.append(based(offsets[s, 0], WLAT))
        lon_base.append(based(offsets[s, 1], WLON))
    first_in = shift(seeded, lat_base[0], lon_base[0])
    first = attend(first_in, 0, offsets, wqkv, wout, norm_gain)
    passed = lax.ppermute(first, "segment", [(0, 1)]).reshape(latents.shape)
    second_in = shift(passed, lat_base[1] - lat_base[0], lon_base[1] - lon_base[0])
    second = attend(second_in, 1, offsets, wqkv, wout, norm_gain)
    merged = jnp.where(segment_index == 0, first, second).reshape(latents.shape)
    return shift_each(merged, [-x for x in lat_base], [-x for x in lon_base])[None]


def solution(mesh):
    return jax.shard_map(
        body,
        mesh=mesh,
        in_specs=(
            P(None, "lat", "lon", None),
            P("lat", "lon"),
            P(),
            P("segment", None, None),
            P("segment", None, None),
            P(),
            P(),
        ),
        out_specs=P("segment", None, "lat", "lon", None),
        check_vma=False,
    )
```

profile of v0, /device:TPU:4, one launch (start us, length us, event | category | flops | bytes accessed | tf_op | source)
XLA Modules:
  0.0 74.3 jit_solution(1935700787173241549)
XLA Ops:
  0.0 1.5 %fusion.19 = (s32[1,1]{1,0:T(1,128)}, s32[1,1]{1,0:T(1,128)}, s32[1,1]{1,0:T(1,128)}, s32[1,1]{1,0:T(1,128)}) fusion(s32[2,2]{1,0:T(2,128)} %offsets_ref.3), kind=kLoop, calls=%fused_computation.62 | loop fusion | bytes 32 | tf_op jit(solution)/shard_map/slice | solution.py:228
  5.5 0.7 broadcast_compare_fusion
  6.2 0.7 convert_element_type.92
  6.9 1.2 %fusion = bf16[2,6,12,1024]{3,2,1,0:T(8,128)(2,1)S(1)} fusion(bf16[2,6,12,1024]{3,0,2,1:T(2,128)(2,1)} %param.23, f32[1024]{0:T(1024)S(1)} %convert_element_type.92, pred[6,12]{1,0:T(8,128)(4,1)S(1)} %broadcast_compare_fusion), kind=kLoop, calls=%fused_computation.13 | loop fusion | flops 589824 | bytes 593992 | tf_op jit(solution)/shard_map/convert_element_type | solution.py:222
  8.1 10.8 %conditional.3 = ((bf16[80,1024]{1,0:T(8,128)(2,1)S(1)}, bf16[48,1024]{1,0:T(8,128)(2,1)S(1)}, bf16[80,1024]{1,0:T(8,128)(2,1)S(1)})) conditional(s32[]{:T(128)} %clamp.10, bf16[2,6,12,1024]{3,2,1,0:T(8,128)(2,1)S(1)} %fusion, bf16[2,6,12,1024]{3,2,1,0:T(8,128)(2,1)S(1)} %fusion, ...), branch_computations={%region_0.1_spmd, %region_1.2_spmd, %region_2.3_spmd, %region_3.4_... | conditional | bytes 2269198 | solution.py:199
  8.2 0.1 slice.206
  8.3 0.1 reshape.209
  8.4 10.4 %branch_3_fun.3 = (bf16[80,1024]{1,0:T(8,128)(2,1)S(1)}, bf16[48,1024]{1,0:T(8,128)(2,1)S(1)}, bf16[80,1024]{1,0:T(8,128)(2,1)S(1)}) custom-call(bf16[80,1024]{1,0:T(8,128)(2,1)S(1)} %pad.107.below_in, bf16[48,1024]{1,0:T(8,128)(2,1)S(1)} %pad.108.corner_in, bf16[80,1024]{1,0:T(8,128)(2,1)S(1)} %pad.109.beside_in), custom_call_target="tpu_custom_call" | custom-call | tf_op jit(solution)/shard_map/cond/branch_3_fun/pallas_call | solution.py:154
  18.9 0.1 reshape.331
  19.1 0.4 fusion.6
  19.5 0.2 fusion.18
  19.8 0.2 fusion.12
  20.0 0.8 %reshape.273.x_ref = bf16[144,1024]{1,0:T(8,128)(2,1)} reshape(bf16[2,6,12,1024]{3,2,1,0:T(8,128)(2,1)S(1)} %fusion.12) | data formatting | bytes 589824 | tf_op jit(solution)/shard_map/reshape | solution.py:88
  20.8 8.8 %shard_map.73 = bf16[144,1024]{1,0:T(8,128)(2,1)} custom-call(s32[2,2]{1,0:T(2,128)} %offsets_ref.3, bf16[144,1024]{1,0:T(8,128)(2,1)} %reshape.273.x_ref, bf16[1024,3072]{1,0:T(8,128)(2,1)} %bitcast.9, bf16[1024,3072]{1,0:T(8,128)(2,1)} %bitcast.10, bf16[1024,3072]{1,0:T(8,128)(2,1)} %bitcast.11, bf16[1024,1024]{1,0:T(8,128)(2,1)} %bitcast.15, ...), custom_call_target="tpu_custom_call" | custom-call | flops 1207959552 | bytes 8388608 | tf_op jit(solution)/shard_map/pallas_call | solution.py:93
  29.6 1.3 %collective-permute-start = (bf16[144,1024]{1,0:T(8,128)(2,1)}, bf16[144,1024]{1,0:T(8,128)(2,1)S(1)}, u32[]{:S(2)}, u32[]{:S(2)}) collective-permute-start(bf16[144,1024]{1,0:T(8,128)(2,1)} %shard_map.73), channel_id=1, source_target_pairs={{0,16},{1,17},{2,18},{3,19},{4,20},{5,21},{6,22},{7,23},{8,24},{9,... | collective-permute-start | bytes 884744 | tf_op jit(solution)/shard_map/ppermute | solution.py:231
  34.7 6.4 %collective-permute-done = bf16[144,1024]{1,0:T(8,128)(2,1)S(1)} collective-permute-done((bf16[144,1024]{1,0:T(8,128)(2,1)}, bf16[144,1024]{1,0:T(8,128)(2,1)S(1)}, u32[]{:S(2)}, u32[]{:S(2)}) %collective-permute-start) | collective-permute-done | bytes 294944 | tf_op jit(solution)/shard_map/ppermute | solution.py:231
  41.1 0.1 reshape.274
  41.2 9.0 %conditional.4 = ((bf16[80,1024]{1,0:T(8,128)(2,1)S(1)}, bf16[48,1024]{1,0:T(8,128)(2,1)S(1)}, bf16[80,1024]{1,0:T(8,128)(2,1)S(1)})) conditional(s32[]{:T(128)} %clamp.11, bf16[2,6,12,1024]{3,2,1,0:T(8,128)(2,1)S(1)} %reshape.274, bf16[2,6,12,1024]{3,2,1,0:T(8,128)(2,1)S(1)} %reshape.274, ...), branch_computations={%region_4.5_spmd, %region_5.6_spmd, %region_6.7_spmd, %region_7.8_... | conditional | bytes 2269198 | solution.py:199
  41.4 0.1 reshape.212
  41.5 8.7 %branch_0_fun.4 = (bf16[80,1024]{1,0:T(8,128)(2,1)S(1)}, bf16[48,1024]{1,0:T(8,128)(2,1)S(1)}, bf16[80,1024]{1,0:T(8,128)(2,1)S(1)}) custom-call(bf16[80,1024]{1,0:T(8,128)(2,1)S(1)} %pad.110.below_in, bf16[48,1024]{1,0:T(8,128)(2,1)S(1)} %pad.111.corner_in, bf16[80,1024]{1,0:T(8,128)(2,1)S(1)} %pad.112.beside_in), custom_call_target="tpu_custom_call" | custom-call | tf_op jit(solution)/shard_map/cond/branch_0_fun/pallas_call | solution.py:154
  50.2 0.1 reshape.334
  50.4 0.4 fusion.4
  50.8 0.2 fusion.16
  51.1 0.2 fusion.10
  51.3 0.8 %reshape.278.x_ref = bf16[144,1024]{1,0:T(8,128)(2,1)} reshape(bf16[2,6,12,1024]{3,2,1,0:T(8,128)(2,1)S(1)} %fusion.10) | data formatting | bytes 589824 | tf_op jit(solution)/shard_map/reshape | solution.py:88
  52.1 0.0 copy-start
  52.1 8.8 %shard_map.74 = bf16[144,1024]{1,0:T(8,128)(2,1)} custom-call(s32[2,2]{1,0:T(2,128)} %offsets_ref.3, bf16[144,1024]{1,0:T(8,128)(2,1)} %reshape.278.x_ref, bf16[1024,3072]{1,0:T(8,128)(2,1)} %bitcast.12, bf16[1024,3072]{1,0:T(8,128)(2,1)} %bitcast.13, bf16[1024,3072]{1,0:T(8,128)(2,1)} %bitcast.14, bf16[1024,1024]{1,0:T(8,128)(2,1)} %bitcast.16, ...), custom_call_target="tpu_custom_call" | custom-call | flops 1207959552 | bytes 8388608 | tf_op jit(solution)/shard_map/pallas_call | solution.py:93
  60.9 0.0 copy-done
  61.0 1.0 %broadcast_select_fusion = bf16[144,1024]{1,0:T(8,128)(2,1)S(1)} fusion(bf16[144,1024]{1,0:T(8,128)(2,1)S(1)} %copy-done, bf16[144,1024]{1,0:T(8,128)(2,1)} %shard_map.74, pred[]{:T(512)S(6)} %eq.28), kind=kLoop, calls=%fused_computation.54 | loop fusion | flops 147456 | bytes 884737 | tf_op jit(solution)/shard_map/jit(_where)/select_n | solution.py:234
  61.9 0.1 reshape.279
  62.0 10.1 %conditional.5 = ((bf16[80,1024]{1,0:T(8,128)(2,1)S(1)}, bf16[48,1024]{1,0:T(8,128)(2,1)S(1)}, bf16[80,1024]{1,0:T(8,128)(2,1)S(1)})) conditional(s32[]{:T(128)} %clamp.9, bf16[2,6,12,1024]{3,2,1,0:T(8,128)(2,1)S(1)} %reshape.279, bf16[2,6,12,1024]{3,2,1,0:T(8,128)(2,1)S(1)} %reshape.279, ...), branch_computations={%region_8.9_spmd, %region_9.10_spmd, %region_10.11_spmd, %region_1... | conditional | flops 184324 | bytes 2637882 | solution.py:213
  62.2 0.1 reshape.235
  62.3 9.8 %branch_0_fun.5 = (bf16[80,1024]{1,0:T(8,128)(2,1)S(1)}, bf16[48,1024]{1,0:T(8,128)(2,1)S(1)}, bf16[80,1024]{1,0:T(8,128)(2,1)S(1)}) custom-call(bf16[80,1024]{1,0:T(8,128)(2,1)S(1)} %pad.122.below_in, bf16[48,1024]{1,0:T(8,128)(2,1)S(1)} %pad.123.corner_in, bf16[80,1024]{1,0:T(8,128)(2,1)S(1)} %pad.124.beside_in), custom_call_target="tpu_custom_call" | custom-call | tf_op jit(solution)/shard_map/cond/branch_0_fun/pallas_call | solution.py:154
  72.2 0.1 reshape.337
  72.4 0.4 fusion.2
  72.8 0.2 fusion.14
  73.1 0.2 fusion.8
  73.3 1.0 %copy.15 = bf16[2,6,12,1024]{3,0,2,1:T(2,128)(2,1)} copy(bf16[2,6,12,1024]{3,2,1,0:T(8,128)(2,1)S(1)} %fusion.8) | data formatting | bytes 589824 | tf_op jit(solution)/shard_map/dynamic_slice | solution.py:190
  (38 shorter events, 0.7 us)
Async XLA Ops:
  29.6 11.5 %collective-permute-start = (bf16[144,1024]{1,0:T(8,128)(2,1)}, bf16[144,1024]{1,0:T(8,128)(2,1)S(1)}, u32[]{:S(2)}, u32[]{:S(2)}) collective-permute-start(bf16[144,1024]{1,0:T(8,128)(2,1)} %shard_map.73), channel_id=1, source_target_pairs={{0,16},{1,17},{2,18},{3,19},{4,20},{5,21},{6,22},{7,23},{8,24},{9,... | collective-permute-start | bytes 884744 | tf_op jit(solution)/shard_map/ppermute | solution.py:231
  52.1 8.8 %copy-start = (bf16[144,1024]{1,0:T(8,128)(2,1)S(1)}, bf16[144,1024]{1,0:T(8,128)(2,1)}, u32[]{:S(2)}) copy-start(bf16[144,1024]{1,0:T(8,128)(2,1)} %shard_map.73) | copy-start | bytes 884740
where the time goes:
time: 75.7 us; the launch traced here: 74.3 us
  Pallas kernels  46.6 us (62%)
  between operations  8.05 us (11%)
  waiting for transfers between devices  6.41 us (8%)
  other arithmetic  6.35 us (8%)
  local copies, waits for them, and re-layouts  5.32 us (7%)
  starting transfers between devices  1.28 us (2%)
    pallas_call x3, Pallas kernels, exchanged(): pl.pallas_call(functools.partial(exchange_kernel, lat_steps, lon_steps),...  28.9 us
    pallas_call x2, Pallas kernels, attend(): pl.pallas_call(functools.partial(attend_kernel, section, head_size=head_s...  17.6 us
    ppermute x1, waiting for transfers between devices, body(): passed = lax.ppermute(first, 'segment', [(0, 1)]).reshape(latents.shape)  6.41 us
    reshape x2, local copies, waits for them, and re-layouts, attend(): flat = field.reshape(-1, width)  1.56 us
  transfers between devices with their start and end apart: 1, of which 1 were waited for; matrix products, arithmetic and copies ran while one was open for 0% of the time, Pallas kernels for 0%

commit v1 on v0

v1 whole, which is shorter than its diff:
```python
import functools
import math

import jax
import jax.numpy as jnp
from jax import lax
from jax.experimental import pallas as pl
from jax.experimental.pallas import tpu as pltpu
from jax.sharding import PartitionSpec as P

HEADS = 16
WLAT = 6
WLON = 12
HALF_LAT = WLAT // 2
HALF_LON = WLON // 2
CELLS = WLAT * WLON
QUAD = 16
PAIR = 128
NT = (((1,), (1,)), ((), ()))
F32 = jnp.float32
BF16 = jnp.bfloat16


def dot(a, b):
    return jnp.dot(a, b, preferred_element_type=F32)


def iota(shape, axis):
    return lax.broadcasted_iota(jnp.int32, shape, axis)


def based(offset, window):
    return jnp.where(offset >= window // 2, offset - window, offset)


def split_by(value, size, count):
    high = sum((value >= size * k).astype(jnp.int32) for k in range(1, count))
    return high, value - size * high


def quarter_cell(t):
    late = t >= 4 * QUAD
    quarter = jnp.where(late, (t - 4 * QUAD) >> 1, t >> 4)
    j = jnp.where(late, QUAD + (t & 1), t & (QUAD - 1))
    row, column = split_by(j, HALF_LON, 3)
    return HALF_LAT * (quarter >> 1) + row, HALF_LON * (quarter & 1) + column


def source(row, column, lat_sign, lon_sign):
    row_out = (row < 0) | (row >= WLAT)
    column_out = (column < 0) | (column >= WLON)
    row = jnp.where(row_out, row - WLAT * lat_sign, row)
    column = jnp.where(column_out, column - WLON * lon_sign, column)
    low, row = split_by(row, HALF_LAT, 2)
    right, column = split_by(column, HALF_LON, 2)
    base = jnp.where(
        row_out,
        jnp.where(column_out, 8 * QUAD, 4 * QUAD + QUAD * right),
        jnp.where(column_out, 6 * QUAD + QUAD * low, 2 * QUAD * low + QUAD * right),
    )
    return base, HALF_LON * row + column


def choosers(row, column, lat_sign, lon_sign, pieces, main_ref, tail_ref):
    base, j = source(row, column, lat_sign, lon_sign)
    count = row.shape[0]
    lane = iota((count, 9 * QUAD), 1)
    main_ref[...] = (lane == jnp.where(j < QUAD, base + j, -1)).astype(F32).astype(BF16)
    tail = jnp.where(j >= QUAD, base + j - QUAD, -1000)
    for piece in range(pieces):
        tail_ref[pl.ds(piece * count, count), :] = (lane == tail + 2 * piece).astype(F32).astype(BF16)


def gathered(block, main_ref, tail_ref, width, pieces):
    count = main_ref.shape[0]
    tail = dot(tail_ref[...], block[:, width:])
    tail = jnp.concatenate([tail[p * count : (p + 1) * count] for p in range(pieces)], axis=1)
    return dot(main_ref[...], block[:, :width]) + tail


def store_quarters(cells, ref, level, width, pieces):
    piece = width // pieces
    ref[level, pl.ds(0, 4 * QUAD), pl.ds(0, width)] = cells[: 4 * QUAD].astype(BF16)
    stack = jnp.concatenate([cells[4 * QUAD :, p * piece : (p + 1) * piece] for p in range(pieces)], axis=0)
    to, at = iota((4 * QUAD, 8 * pieces), 0), iota((4 * QUAD, 8 * pieces), 1)
    wanted = 8 * ((to & (QUAD - 1)) >> 1) + 2 * (to >> 4) + (to & 1)
    pick = (at == wanted).astype(F32).astype(BF16)
    ref[level, pl.ds(0, 4 * QUAD), pl.ds(width, piece)] = dot(pick, stack.astype(BF16)).astype(BF16)


def seeded_cells(level, latents_ref, mask_ref, embed_ref):
    embed = embed_ref[...].astype(F32)
    diagonal = iota((WLON, WLON), 0) == iota((WLON, WLON), 1)
    rows = []
    for row in range(WLAT):
        land = jnp.where(diagonal, mask_ref[row : row + 1, :].astype(F32), 0.0)
        land = jnp.sum(land, axis=1, keepdims=True)
        rows.append(latents_ref[level, row].astype(F32) + land * embed)
    cells = jnp.concatenate(rows, axis=0).astype(BF16)
    row, column = quarter_cell(iota((CELLS, CELLS), 0))
    order = (iota((CELLS, CELLS), 1) == WLON * row + column).astype(F32).astype(BF16)
    return dot(order, cells)


def attended(q, k, v, bias, head_size):
    cells = q.shape[0]
    first = iota((cells, PAIR), 1) < head_size
    ones = jnp.ones((cells, PAIR), BF16)
    pairs = [slice(p * PAIR, (p + 1) * PAIR) for p in range(q.shape[1] // PAIR)]
    scores = []
    for pair in pairs:
        zero = jnp.zeros((cells, PAIR), F32)
        both = jnp.concatenate([jnp.where(first, q[:, pair], zero), jnp.where(first, zero, q[:, pair])], axis=0)
        scores.append(lax.dot_general(both.astype(BF16), k[:, pair].astype(BF16), NT, preferred_element_type=F32))
    weights = []
    for score in scores:
        score = score + bias
        weights.append(jnp.exp(score - jnp.max(score, axis=-1, keepdims=True)).astype(BF16))
    sums = [
        dot(weight, jnp.concatenate([v[:, pair].astype(BF16), ones], axis=1))
        for weight, pair in zip(weights, pairs)
    ]
    parts = []
    for both in sums:
        value = jnp.where(first, both[:cells, :PAIR], both[cells:, :PAIR])
        total = jnp.where(first, both[:cells, PAIR:], both[cells:, PAIR:])
        parts.append((value / total).astype(BF16))
    return jnp.concatenate(parts, axis=1)


def section(x, bias, wqkv, wout, gain):
    width = x.shape[1]
    head_size = width // HEADS
    q = dot(x, wqkv[:, :width]) * (1.0 / math.sqrt(head_size))
    k = dot(x, wqkv[:, width : 2 * width])
    v = dot(x, wqkv[:, 2 * width :])
    projected = dot(attended(q, k, v, bias, head_size), wout[...])
    centered = projected - jnp.mean(projected, axis=-1, keepdims=True)
    variance = jnp.mean(centered * centered, axis=-1, keepdims=True)
    branch = centered * lax.rsqrt(variance + 1e-05) * gain
    return x.astype(F32) + branch


def kernel(
    lat_signs, lon_signs,
    offsets_ref, latents_ref, mask_ref, embed_ref, wqkv_hbm, wout_hbm, gain_ref, out_ref,
    entering, leaving, wqkv, wout, main_in, tail_in, main_out, tail_out, bias,
    weight_sem, send_sem, recv_sem, cross_send, cross_recv,
):
    segment, lon, lat = (lax.axis_index(axis) for axis in ("segment", "lon", "lat"))
    lons, lats = lax.axis_size("lon"), lax.axis_size("lat")
    levels = latents_ref.shape[0]
    width = latents_ref.shape[-1]
    pieces = width // PAIR
    at = lambda a, b: (segment, lax.rem(lon + b + lons, lons), lax.rem(lat + a + lats, lats))
    pick = lambda pair: pair[0] + segment * (pair[1] - pair[0])

    loads = [
        pltpu.make_async_copy(wqkv_hbm.at[0], wqkv, weight_sem.at[0]),
        pltpu.make_async_copy(wout_hbm.at[0], wout, weight_sem.at[1]),
    ]
    for load in loads:
        load.start()
    across = (1 - segment, lon, lat)
    partners = [at(a, b) for a in (-1, 0, 1) for b in (-1, 0, 1) if (a, b) != (0, 0)] + [across]
    barrier = pltpu.get_barrier_semaphore()
    for partner in partners:
        pl.semaphore_signal(barrier, inc=1, device_id=partner, device_id_type=pl.DeviceIdType.MESH)

    def exchange(index, ref, level):
        a, b = pick(lat_signs[index]), pick(lon_signs[index])
        low, right = (1 - a) // 2, (1 - b) // 2
        plan = (
            (2 * QUAD * low, 2 * QUAD, 4 * QUAD, at(-a, 0)),
            (QUAD * right, QUAD, 6 * QUAD, at(0, -b)),
            (2 * QUAD + QUAD * right, QUAD, 7 * QUAD, at(0, -b)),
            (2 * QUAD * low + QUAD * right, QUAD, 8 * QUAD, at(-a, -b)),
        )
        return [
            pltpu.make_async_remote_copy(
                src_ref=ref.at[level, pl.ds(pl.multiple_of(start, QUAD), count)],
                dst_ref=ref.at[level, pl.ds(target, count)],
                send_sem=send_sem.at[index, level, slot],
                recv_sem=recv_sem.at[index, level, slot],
                device_id=device,
                device_id_type=pl.DeviceIdType.MESH,
            )
            for slot, (start, count, target, device) in enumerate(plan)
        ]

    def crossing(level):
        return pltpu.make_async_remote_copy(
            src_ref=leaving.at[level, pl.ds(0, 4 * QUAD)],
            dst_ref=entering.at[level, pl.ds(0, 4 * QUAD)],
            send_sem=cross_send.at[level],
            recv_sem=cross_recv.at[level],
            device_id=across,
            device_id_type=pl.DeviceIdType.MESH,
        )

    def each_level(step):
        def run(level, carry):
            step(level)
            return carry

        lax.fori_loop(0, levels, run, 0)

    @pl.when(segment == 0)
    def _():
        def seed(level):
            store_quarters(seeded_cells(level, latents_ref, mask_ref, embed_ref), entering, level, width, pieces)

        each_level(seed)

    pl.semaphore_wait(barrier, len(partners))

    def enter(level):
        for copy in exchange(0, entering, level):
            copy.start()

    @pl.when(segment == 0)
    def _():
        each_level(enter)

    lat_base = [based(offsets_ref[s, 0], WLAT) for s in (0, 1)]
    lon_base = [based(offsets_ref[s, 1], WLON) for s in (0, 1)]
    first = segment == 0
    lat_own, lon_own = jnp.where(first, lat_base[0], lat_base[1]), jnp.where(first, lon_base[0], lon_base[1])
    lat_in = jnp.where(first, lat_base[0], lat_base[1] - lat_base[0])
    lon_in = jnp.where(first, lon_base[0], lon_base[1] - lon_base[0])
    offset = jnp.where(first, offsets_ref[0, 0], offsets_ref[1, 0])

    row, column = quarter_cell(iota((CELLS, 1), 0))
    choosers(row + lat_in, column + lon_in, pick(lat_signs[0]), pick(lon_signs[0]), pieces, main_in, tail_in)
    line = iota((WLAT * QUAD, 1), 0)
    row, column = line >> 4, jnp.minimum(line & (QUAD - 1), WLON - 1)
    choosers(row - lat_own, column - lon_own, pick(lat_signs[1]), pick(lon_signs[1]), pieces, main_out, tail_out)

    def wrapped(shape, axis):
        row, _ = quarter_cell(iota(shape, axis))
        held = lat * WLAT + lat_own + row
        held = jnp.where(held < 0, held + lats * WLAT, held)
        held = jnp.where(held >= lats * WLAT, held - lats * WLAT, held)
        return (held < offset).astype(jnp.int32)

    excluded = jnp.where(wrapped((CELLS, 1), 0) == wrapped((1, CELLS), 1), 0.0, -1e30)
    bias[pl.ds(0, CELLS), :] = excluded
    bias[pl.ds(CELLS, CELLS), :] = excluded
    for load in loads:
        load.wait()

    @pl.when(segment == 1)
    def _():
        def forward(level):
            crossing(level).wait_recv()
            enter(level)

        each_level(forward)

    gain = jnp.where(first, gain_ref[0:1, :], gain_ref[1:2, :])

    def work(level):
        for copy in exchange(0, entering, level):
            copy.wait_recv()
        x = gathered(entering[level], main_in, tail_in, width, pieces).astype(BF16)
        store_quarters(section(x, bias[...], wqkv, wout, gain), leaving, level, width, pieces)

        @pl.when(segment == 0)
        def _():
            crossing(level).start()

        for copy in exchange(1, leaving, level):
            copy.start()

    each_level(work)

    def finish(level):
        for copy in exchange(1, leaving, level):
            copy.wait_recv()
        cells = gathered(leaving[level], main_out, tail_out, width, pieces).astype(BF16)
        for row in range(WLAT):
            out_ref[0, level, row] = cells[row * QUAD : row * QUAD + WLON]

    each_level(finish)

    def settle(level):
        for index, ref in enumerate((entering, leaving)):
            for copy in exchange(index, ref, level):
                copy.wait_send()

        @pl.when(segment == 0)
        def _():
            crossing(level).wait_send()

    each_level(settle)


def sections(variant, offsets, latents, land_mask, land_embed, qkv_weight, out_weight, norm_gain):
    levels, _, _, width = latents.shape
    second_known = variant >= 4
    signs = []
    for bit in (2, 1):
        other = -1 if variant & bit else 1
        if second_known:
            entering, leaving = (other, -other), (-other, 1)
        else:
            entering, leaving = (-1, other), (1, -other)
        signs.append((entering, leaving))
    pieces = width // PAIR
    in_vmem = pl.BlockSpec(memory_space=pltpu.VMEM)
    in_hbm = pl.BlockSpec(memory_space=pl.ANY)
    block = (levels, 9 * QUAD, width + PAIR)
    return pl.pallas_call(
        functools.partial(kernel, signs[0], signs[1]),
        out_shape=jax.ShapeDtypeStruct((1,) + latents.shape, BF16),
        in_specs=[pl.BlockSpec(memory_space=pltpu.SMEM), in_vmem, in_vmem, in_vmem, in_hbm, in_hbm, in_vmem],
        out_specs=in_vmem,
        scratch_shapes=[
            pltpu.VMEM(block, BF16),
            pltpu.VMEM(block, BF16),
            pltpu.VMEM(qkv_weight.shape[1:], BF16),
            pltpu.VMEM(out_weight.shape[1:], BF16),
            pltpu.VMEM((CELLS, 9 * QUAD), BF16),
            pltpu.VMEM((CELLS * pieces, 9 * QUAD), BF16),
            pltpu.VMEM((WLAT * QUAD, 9 * QUAD), BF16),
            pltpu.VMEM((WLAT * QUAD * pieces, 9 * QUAD), BF16),
            pltpu.VMEM((2 * CELLS, CELLS), F32),
            pltpu.SemaphoreType.DMA((2,)),
            pltpu.SemaphoreType.DMA((2, levels, 4)),
            pltpu.SemaphoreType.DMA((2, levels, 4)),
            pltpu.SemaphoreType.DMA((levels,)),
            pltpu.SemaphoreType.DMA((levels,)),
        ],
        compiler_params=pltpu.CompilerParams(
            collective_id=variant, has_side_effects=True, vmem_limit_bytes=48 * 1024 * 1024
        ),
    )(offsets, latents, land_mask, land_embed, qkv_weight, out_weight, norm_gain)


def body(latents, land_mask, land_embed, qkv_weight, out_weight, norm_gain, offsets):
    assert latents.shape[1:3] == (WLAT, WLON)
    window = jnp.array([[WLAT, WLON]], jnp.int32)
    negative = (2 * offsets >= window).astype(jnp.int32) * jnp.array([[2, 1], [8, 4]], jnp.int32)
    unusual = (offsets[0:1] != window - 1).astype(jnp.int32) * 16
    code = jnp.sum(negative + jnp.pad(unusual, ((0, 1), (0, 0))))
    variant = jnp.where(code >= 16, 4 + (code & 3), (code >> 2) & 3)
    ways = [functools.partial(sections, v) for v in range(8)]
    return lax.switch(
        variant, ways, offsets, latents, land_mask, land_embed.reshape(1, -1), qkv_weight, out_weight, norm_gain
    )


def solution(mesh):
    return jax.shard_map(
        body,
        mesh=mesh,
        in_specs=(
            P(None, "lat", "lon", None),
            P("lat", "lon"),
            P(),
            P("segment", None, None),
            P("segment", None, None),
            P(),
            P(),
        ),
        out_specs=P("segment", None, "lat", "lon", None),
        check_vma=False,
    )
```

time: 75.7 us -> 40.6 us (0.54)
  the two profiles are of different devices: /device:TPU:4 before, /device:TPU:5 now
where the time goes in v1:
time: 40.6 us; the launch traced here: 41 us
  Pallas kernels  34.1 us (84%)
  local copies, waits for them, and re-layouts  2.73 us (7%)
  other arithmetic  2.03 us (5%)
  between operations  1.97 us (5%)
    pallas_call x1, Pallas kernels, sections(): pl.pallas_call(functools.partial(kernel, signs[0], signs[1]), out_shape=j...  34.1 us
    reduce_sum x1, other arithmetic, body(): code = jnp.sum(negative + jnp.pad(unusual, ((0, 1), (0, 0))))  1.34 us
    another operation x1, local copies, waits for them, and re-layouts  1.03 us

profile of v1, /device:TPU:5, one launch (start us, length us, event | category | flops | bytes accessed | tf_op | source)
XLA Modules:
  0.0 41.0 jit_solution(4614217579820598588)
XLA Ops:
  0.0 0.7 %compare_select_fusion = s32[1,2]{1,0:T(1,128)S(1)} fusion(s32[1,2]{1,0:T(1,128)} %constant.32, s32[2,2]{1,0:T(2,128)} %param.23), kind=kLoop, calls=%fused_computation | loop fusion | flops 4 | bytes 24 | tf_op jit(solution)/shard_map/mul | solution.py:344
  0.7 1.3 %fusion.1 = s32[]{:T(128)} fusion(s32[2,2]{1,0:T(2,128)} %constant.24.clone, s32[1,2]{1,0:T(1,128)S(1)} %compare_select_fusion, s32[2,2]{1,0:T(2,128)} %param.23, s32[2]{0:T(128)} %constant.31), kind=kLoop, calls=%fused_computation.3 | loop fusion | flops 19 | bytes 52 | tf_op jit(solution)/shard_map/reduce_sum | solution.py:345
  4.0 0.7 %reshape.3 = bf16[1,1024]{1,0:T(2,128)(2,1)S(1)} reshape(bf16[1024]{0:T(1024)(128)(2,1)} %param.19) | data formatting | bytes 4096 | tf_op jit(solution)/shard_map/reshape | solution.py:349
  4.7 35.6 %conditional.1 = (bf16[1,2,6,12,1024]{4,1,3,2,0:T(2,128)(2,1)S(1)}) conditional(s32[]{:T(128)} %clamp.3, (s32[2,2]{1,0:T(2,128)}, bf16[2,6,12,1024]{3,0,2,1:T(2,128)(2,1)}, s32[6,12]{1,0:T(8,128)}, bf16[1,1024]{1,0:T(2,128)(2,1)S(1)}, bf16[1,1024,3072]{2,1,0:T(8,128)(2,1)}, ...), branch_computations={%region_1.2_spmd, %region_2.3_spmd, %region_3.4_spmd, %region_4.5_... | conditional | bytes 1179656 | solution.py:348
  4.7 1.0 %copy.19.latents_ref = bf16[2,6,12,1024]{3,2,1,0:T(8,128)(2,1)S(1)} copy(bf16[2,6,12,1024]{3,0,2,1:T(2,128)(2,1)} %get-tuple-element.191) | data formatting | bytes 589824 | tf_op jit(solution)/shard_map
  5.7 34.1 %branch_1_fun.1 = bf16[1,2,6,12,1024]{4,3,2,1,0:T(8,128)(2,1)S(1)} custom-call(s32[2,2]{1,0:T(2,128)} %get-tuple-element.133.offsets_ref, bf16[2,6,12,1024]{3,2,1,0:T(8,128)(2,1)S(1)} %copy.19.latents_ref, s32[6,12]{1,0:T(8,128)} %get-tuple-element.135.mask_ref, bf16[1,1024]{1,0:T(2,128)(2,1)S(1)} %get-tuple-element.136.embed_ref, ...), custom_call_target="tpu_custom_call" | custom-call | tf_op jit(solution)/shard_map/cond/branch_1_fun/pallas_call | solution.py:313
  39.8 0.3 copy.28
  40.3 0.0 copy-start
  40.3 0.7 %copy-done = bf16[1,2,6,12,1024]{4,1,3,2,0:T(2,128)(2,1)} copy-done((bf16[1,2,6,12,1024]{4,1,3,2,0:T(2,128)(2,1)}, bf16[1,2,6,12,1024]{4,1,3,2,0:T(2,128)(2,1)S(1)}, u32[]{:S(2)}) %copy-start) | copy-done | bytes 294936
Async XLA Ops:
  40.3 0.7 %copy-start = (bf16[1,2,6,12,1024]{4,1,3,2,0:T(2,128)(2,1)}, bf16[1,2,6,12,1024]{4,1,3,2,0:T(2,128)(2,1)S(1)}, u32[]{:S(2)}) copy-start(bf16[1,2,6,12,1024]{4,1,3,2,0:T(2,128)(2,1)S(1)} %get-tuple-element.248) | copy-start | bytes 884740

commit v2 on v1

--- a/solution.py
+++ b/solution.py
@@ -61,11 +61,13 @@
     return base, HALF_LON * row + column
 
 
-def choosers(row, column, lat_sign, lon_sign, pieces, main_ref, tail_ref):
+def choosers(row, column, lat_sign, lon_sign, pieces, main_ref, tail_ref, wanted=None):
     base, j = source(row, column, lat_sign, lon_sign)
+    if wanted is not None:
+        base = jnp.where(wanted, base, -2000)
     count = row.shape[0]
     lane = iota((count, 9 * QUAD), 1)
-    main_ref[...] = (lane == jnp.where(j < QUAD, base + j, -1)).astype(F32).astype(BF16)
+    main_ref[...] = (lane == jnp.where(j < QUAD, base + j, -1000)).astype(F32).astype(BF16)
     tail = jnp.where(j >= QUAD, base + j - QUAD, -1000)
     for piece in range(pieces):
         tail_ref[pl.ds(piece * count, count), :] = (lane == tail + 2 * piece).astype(F32).astype(BF16)
@@ -79,6 +81,7 @@
 
 
 def store_quarters(cells, ref, level, width, pieces):
+    cells = cells.astype(F32)
     piece = width // pieces
     ref[level, pl.ds(0, 4 * QUAD), pl.ds(0, width)] = cells[: 4 * QUAD].astype(BF16)
     stack = jnp.concatenate([cells[4 * QUAD :, p * piece : (p + 1) * piece] for p in range(pieces)], axis=0)
@@ -88,18 +91,24 @@
     ref[level, pl.ds(0, 4 * QUAD), pl.ds(width, piece)] = dot(pick, stack.astype(BF16)).astype(BF16)
 
 
-def seeded_cells(level, latents_ref, mask_ref, embed_ref):
-    embed = embed_ref[...].astype(F32)
-    diagonal = iota((WLON, WLON), 0) == iota((WLON, WLON), 1)
+def seed(entering, latents_ref, mask_ref, embed_ref, pieces):
+    levels, width = latents_ref.shape[2:]
+    embed = embed_ref[...].astype(F32).reshape(1, width)
+    across = WLON * levels
+    spread = iota((across, WLON), 0)
+    spread = (spread >= levels * iota((across, WLON), 1)) & (spread < levels * iota((across, WLON), 1) + levels)
     rows = []
     for row in range(WLAT):
-        land = jnp.where(diagonal, mask_ref[row : row + 1, :].astype(F32), 0.0)
+        land = jnp.where(spread, mask_ref[row : row + 1, :].astype(F32), 0.0)
         land = jnp.sum(land, axis=1, keepdims=True)
-        rows.append(latents_ref[level, row].astype(F32) + land * embed)
+        rows.append(latents_ref[row].astype(F32).reshape(across, width) + land * embed)
     cells = jnp.concatenate(rows, axis=0).astype(BF16)
-    row, column = quarter_cell(iota((CELLS, CELLS), 0))
-    order = (iota((CELLS, CELLS), 1) == WLON * row + column).astype(F32).astype(BF16)
-    return dot(order, cells)
+    row, column = quarter_cell(iota((CELLS, CELLS * levels), 0))
+    wanted = levels * (WLON * row + column)
+    at = iota((CELLS, CELLS * levels), 1)
+    for level in range(levels):
+        order = (at == wanted + level).astype(F32).astype(BF16)
+        store_quarters(dot(order, cells), entering, level, width, pieces)
 
 
 def attended(q, k, v, bias, head_size):
@@ -144,13 +153,12 @@
 def kernel(
     lat_signs, lon_signs,
     offsets_ref, latents_ref, mask_ref, embed_ref, wqkv_hbm, wout_hbm, gain_ref, out_ref,
-    entering, leaving, wqkv, wout, main_in, tail_in, main_out, tail_out, bias,
+    entering, leaving, wqkv, wout, main_in, tail_in, main_out, tail_out, bias, total,
     weight_sem, send_sem, recv_sem, cross_send, cross_recv,
 ):
     segment, lon, lat = (lax.axis_index(axis) for axis in ("segment", "lon", "lat"))
     lons, lats = lax.axis_size("lon"), lax.axis_size("lat")
-    levels = latents_ref.shape[0]
-    width = latents_ref.shape[-1]
+    levels, width = latents_ref.shape[2:]
     pieces = width // PAIR
     at = lambda a, b: (segment, lax.rem(lon + b + lons, lons), lax.rem(lat + a + lats, lats))
     pick = lambda pair: pair[0] + segment * (pair[1] - pair[0])
@@ -188,12 +196,15 @@
             for slot, (start, count, target, device) in enumerate(plan)
         ]
 
-    def crossing(level):
+    low_next = (1 - lat_signs[0][1]) // 2
+
+    def crossing(level, part):
+        rows = pl.ds(2 * QUAD * (low_next if part == 0 else 1 - low_next), 2 * QUAD)
         return pltpu.make_async_remote_copy(
-            src_ref=leaving.at[level, pl.ds(0, 4 * QUAD)],
-            dst_ref=entering.at[level, pl.ds(0, 4 * QUAD)],
-            send_sem=cross_send.at[level],
-            recv_sem=cross_recv.at[level],
+            src_ref=leaving.at[level, rows],
+            dst_ref=entering.at[level, rows],
+            send_sem=cross_send.at[level, part],
+            recv_sem=cross_recv.at[level, part],
             device_id=across,
             device_id_type=pl.DeviceIdType.MESH,
         )
@@ -207,10 +218,7 @@
 
     @pl.when(segment == 0)
     def _():
-        def seed(level):
-            store_quarters(seeded_cells(level, latents_ref, mask_ref, embed_ref), entering, level, width, pieces)
-
-        each_level(seed)
+        seed(entering, latents_ref, mask_ref, embed_ref, pieces)
 
     pl.semaphore_wait(barrier, len(partners))
 
@@ -232,9 +240,14 @@
 
     row, column = quarter_cell(iota((CELLS, 1), 0))
     choosers(row + lat_in, column + lon_in, pick(lat_signs[0]), pick(lon_signs[0]), pieces, main_in, tail_in)
-    line = iota((WLAT * QUAD, 1), 0)
-    row, column = line >> 4, jnp.minimum(line & (QUAD - 1), WLON - 1)
-    choosers(row - lat_own, column - lon_own, pick(lat_signs[1]), pick(lon_signs[1]), pieces, main_out, tail_out)
+    line = iota((CELLS * levels, 1), 0)
+    row, column = split_by(line, WLON * levels, WLAT)
+    column, held_level = split_by(column, levels, WLON)
+    for level in range(levels):
+        choosers(
+            row - lat_own, column - lon_own, pick(lat_signs[1]), pick(lon_signs[1]),
+            pieces, main_out.at[level], tail_out.at[level], held_level == level,
+        )
 
     def wrapped(shape, axis):
         row, _ = quarter_cell(iota(shape, axis))
@@ -252,8 +265,12 @@
     @pl.when(segment == 1)
     def _():
         def forward(level):
-            crossing(level).wait_recv()
-            enter(level)
+            copies = exchange(0, entering, level)
+            crossing(level, 0).wait_recv()
+            for slot in (0, 3, 1 + low_next):
+                copies[slot].start()
+            crossing(level, 1).wait_recv()
+            copies[2 - low_next].start()
 
         each_level(forward)
 
@@ -267,21 +284,23 @@
 
         @pl.when(segment == 0)
         def _():
-            crossing(level).start()
+            for part in (0, 1):
+                crossing(level, part).start()
 
         for copy in exchange(1, leaving, level):
             copy.start()
 
     each_level(work)
+
+    total[...] = jnp.zeros_like(total)
 
     def finish(level):
         for copy in exchange(1, leaving, level):
             copy.wait_recv()
-        cells = gathered(leaving[level], main_out, tail_out, width, pieces).astype(BF16)
-        for row in range(WLAT):
-            out_ref[0, level, row] = cells[row * QUAD : row * QUAD + WLON]
+        total[...] += gathered(leaving[level], main_out.at[level], tail_out.at[level], width, pieces)
 
     each_level(finish)
+    out_ref[...] = total[...].astype(BF16).reshape(out_ref.shape)
 
     def settle(level):
         for index, ref in enumerate((entering, leaving)):
@@ -290,13 +309,14 @@
 
         @pl.when(segment == 0)
         def _():
-            crossing(level).wait_send()
+            for part in (0, 1):
+                crossing(level, part).wait_send()
 
     each_level(settle)
 
 
 def sections(variant, offsets, latents, land_mask, land_embed, qkv_weight, out_weight, norm_gain):
-    levels, _, _, width = latents.shape
+    _, _, levels, width = latents.shape
     second_known = variant >= 4
     signs = []
     for bit in (2, 1):
@@ -312,7 +332,7 @@
     block = (levels, 9 * QUAD, width + PAIR)
     return pl.pallas_call(
         functools.partial(kernel, signs[0], signs[1]),
-        out_shape=jax.ShapeDtypeStruct((1,) + latents.shape, BF16),
+        out_shape=jax.ShapeDtypeStruct(latents.shape, BF16),
         in_specs=[pl.BlockSpec(memory_space=pltpu.SMEM), in_vmem, in_vmem, in_vmem, in_hbm, in_hbm, in_vmem],
         out_specs=in_vmem,
         scratch_shapes=[
@@ -322,14 +342,15 @@
             pltpu.VMEM(out_weight.shape[1:], BF16),
             pltpu.VMEM((CELLS, 9 * QUAD), BF16),
             pltpu.VMEM((CELLS * pieces, 9 * QUAD), BF16),
-            pltpu.VMEM((WLAT * QUAD, 9 * QUAD), BF16),
-            pltpu.VMEM((WLAT * QUAD * pieces, 9 * QUAD), BF16),
+            pltpu.VMEM((levels, CELLS * levels, 9 * QUAD), BF16),
+            pltpu.VMEM((levels, CELLS * levels * pieces, 9 * QUAD), BF16),
             pltpu.VMEM((2 * CELLS, CELLS), F32),
+            pltpu.VMEM((CELLS * levels, width), F32),
             pltpu.SemaphoreType.DMA((2,)),
             pltpu.SemaphoreType.DMA((2, levels, 4)),
             pltpu.SemaphoreType.DMA((2, levels, 4)),
-            pltpu.SemaphoreType.DMA((levels,)),
-            pltpu.SemaphoreType.DMA((levels,)),
+            pltpu.SemaphoreType.DMA((levels, 2)),
+            pltpu.SemaphoreType.DMA((levels, 2)),
         ],
         compiler_params=pltpu.CompilerParams(
             collective_id=variant, has_side_effects=True, vmem_limit_bytes=48 * 1024 * 1024
@@ -339,15 +360,17 @@
 
 def body(latents, land_mask, land_embed, qkv_weight, out_weight, norm_gain, offsets):
     assert latents.shape[1:3] == (WLAT, WLON)
-    window = jnp.array([[WLAT, WLON]], jnp.int32)
-    negative = (2 * offsets >= window).astype(jnp.int32) * jnp.array([[2, 1], [8, 4]], jnp.int32)
-    unusual = (offsets[0:1] != window - 1).astype(jnp.int32) * 16
-    code = jnp.sum(negative + jnp.pad(unusual, ((0, 1), (0, 0))))
-    variant = jnp.where(code >= 16, 4 + (code & 3), (code >> 2) & 3)
+    lat_part, lon_part = offsets[:, 0:1], offsets[:, 1:2]
+    signs = 2 * (lat_part >= HALF_LAT).astype(jnp.int32) + (lon_part >= HALF_LON).astype(jnp.int32)
+    known = (lat_part == WLAT - 1) & (lon_part == WLON - 1)
+    term = jnp.where(iota((2, 1), 0) == 0, jnp.where(known, 0, 1 + signs), signs)
+    variant = jnp.sum(term)
     ways = [functools.partial(sections, v) for v in range(8)]
-    return lax.switch(
-        variant, ways, offsets, latents, land_mask, land_embed.reshape(1, -1), qkv_weight, out_weight, norm_gain
+    out = lax.switch(
+        variant, ways,
+        offsets, latents.transpose(1, 2, 0, 3), land_mask, land_embed, qkv_weight, out_weight, norm_gain,
     )
+    return out.transpose(2, 0, 1, 3)[None]
 
 
 def solution(mesh):

time: 40.6 us -> 34.5 us (0.85); the launches traced: 41 us -> 34.1 us
  Pallas kernels: 34.1 us -> 31 us
  local copies, waits for them, and re-layouts: 2.73 us -> 0.72 us
  between operations: 1.97 us -> 0.66 us
  other arithmetic: 2.03 us -> 1.46 us
    pallas_call x1, Pallas kernels: 34.1 us -> 31 us  [sections(): pl.pallas_call(functools.partial(kernel, signs[0], signs[1]), out_shape=j...]
    another operation x1 -> x0, local copies, waits for them, and re-layouts: 1.03 us -> none
    mul x1 -> x0, other arithmetic: 0.7 us -> none  [body(): unusual = (offsets[0:1] != window - 1).astype(jnp.int32) * 16]
    reshape x1 -> x0, local copies, waits for them, and re-layouts: 0.69 us -> none  [body(): land_embed.reshape(1, -1)]
where the time goes in v2:
time: 34.5 us; the launch traced here: 34.1 us
  Pallas kernels  31 us (90%)
  other arithmetic  1.46 us (4%)
  local copies, waits for them, and re-layouts  0.72 us (2%)
  between operations  0.66 us (2%)
    pallas_call x1, Pallas kernels, sections(): pl.pallas_call(functools.partial(kernel, signs[0], signs[1]), out_shape=j...  31 us
    reduce_sum x1, other arithmetic, body(): variant = jnp.sum(term)  1.46 us
    unnamed x1, local copies, waits for them, and re-layouts  0.72 us

profile of v2, /device:TPU:5, one launch (start us, length us, event | category | flops | bytes accessed | tf_op | source)
XLA Modules:
  0.0 34.1 jit_solution(14297808520341143760)
XLA Ops:
  0.0 1.5 %fusion = s32[]{:T(128)} fusion(s32[2,2]{1,0:T(2,128)} %param.21), kind=kLoop, calls=%fused_computation.4 | loop fusion | flops 25 | bytes 20 | tf_op jit(solution)/shard_map/reduce_sum | solution.py:367
  2.1 31.3 %conditional.1 = (bf16[6,12,2,1024]{3,2,1,0:T(2,128)(2,1)S(1)}) conditional(s32[]{:T(128)} %clamp.3, (s32[2,2]{1,0:T(2,128)}, bf16[6,12,2,1024]{3,2,1,0:T(2,128)(2,1)}, s32[6,12]{1,0:T(8,128)}, bf16[1024]{0:T(1024)(128)(2,1)}, bf16[1,1024,3072]{2,1,0:T(8,128)(2,1)}, /*index=5*/bf16[1,1024,1024]{2,1,0:T(8,128)(2,1)}, ...), branch_computations={%region_1.2_spmd, %region_2.3_spmd, %region_3.4_spmd, %region_4.5_... | conditional | bytes 8 | solution.py:369
  2.3 31.0 %branch_4_fun.1 = bf16[6,12,2,1024]{3,2,1,0:T(2,128)(2,1)S(1)} custom-call(s32[2,2]{1,0:T(2,128)} %get-tuple-element.154.offsets_ref, bf16[6,12,2,1024]{3,2,1,0:T(2,128)(2,1)} %get-tuple-element.155.latents_ref, s32[6,12]{1,0:T(8,128)} %get-tuple-element.156.mask_ref, bf16[1024]{0:T(1024)(128)(2,1)} %get-tuple-element.157.embed_ref, ...), custom_call_target="tpu_custom_call" | custom-call | tf_op jit(solution)/shard_map/cond/branch_4_fun/pallas_call | solution.py:333
  33.4 0.7 %copy.17 = bf16[1,2,6,12,1024]{4,1,3,2,0:T(2,128)(2,1)} copy(bf16[1,2,6,12,1024]{4,1,3,2,0:T(2,128)(2,1)S(1)} %bitcast.12) | data formatting | bytes 589824

commit v3 on v2

--- a/solution.py
+++ b/solution.py
@@ -46,23 +46,30 @@
     return HALF_LAT * (quarter >> 1) + row, HALF_LON * (quarter & 1) + column
 
 
-def source(row, column, lat_sign, lon_sign):
+def source(row, column, lat_sign, lon_sign, small):
     row_out = (row < 0) | (row >= WLAT)
     column_out = (column < 0) | (column >= WLON)
     row = jnp.where(row_out, row - WLAT * lat_sign, row)
     column = jnp.where(column_out, column - WLON * lon_sign, column)
-    low, row = split_by(row, HALF_LAT, 2)
-    right, column = split_by(column, HALF_LON, 2)
+    low, near_row = split_by(row, HALF_LAT, 2)
+    right, near_column = split_by(column, HALF_LON, 2)
     base = jnp.where(
         row_out,
         jnp.where(column_out, 8 * QUAD, 4 * QUAD + QUAD * right),
         jnp.where(column_out, 6 * QUAD + QUAD * low, 2 * QUAD * low + QUAD * right),
     )
-    return base, HALF_LON * row + column
-
-
-def choosers(row, column, lat_sign, lon_sign, pieces, main_ref, tail_ref, wanted=None):
-    base, j = source(row, column, lat_sign, lon_sign)
+    j = HALF_LON * near_row + near_column
+    if small is None:
+        return base, j
+    inside = ~(row_out | column_out)
+    small_base = jnp.where(row_out, jnp.where(column_out, 8 * QUAD, 4 * QUAD), 6 * QUAD)
+    small_j = jnp.where(row_out, jnp.where(column_out, QUAD, column), row)
+    whole = inside | jnp.logical_not(small)
+    return jnp.where(whole, base, small_base), jnp.where(whole, j, small_j)
+
+
+def choosers(row, column, lat_sign, lon_sign, small, pieces, main_ref, tail_ref, wanted=None):
+    base, j = source(row, column, lat_sign, lon_sign, small)
     if wanted is not None:
         base = jnp.where(wanted, base, -2000)
     count = row.shape[0]
@@ -91,7 +98,24 @@
     ref[level, pl.ds(0, 4 * QUAD), pl.ds(width, piece)] = dot(pick, stack.astype(BF16)).astype(BF16)
 
 
-def seed(entering, latents_ref, mask_ref, embed_ref, pieces):
+def store_edges(cells, lat_sign, lon_sign, line_ref, corner_ref, level, pieces):
+    row_at, column_at = (0 if lat_sign > 0 else WLAT - 1), (0 if lon_sign > 0 else WLON - 1)
+    to = iota((2 * QUAD, CELLS), 0)
+    row, column = quarter_cell(iota((2 * QUAD, CELLS), 1))
+    pick = ((row == row_at) & (column == to)) | ((column == column_at) & (row == to - QUAD))
+    line_ref[level] = dot(pick.astype(F32).astype(BF16), cells.astype(BF16)).astype(BF16)
+    half = HALF_LON * (row_at % HALF_LAT) + column_at % HALF_LON
+    quarter = 2 * (row_at // HALF_LAT) + column_at // HALF_LON
+    place = QUAD * quarter + half if half < QUAD else 4 * QUAD + 2 * quarter + half - QUAD
+    piece = cells.shape[1] // pieces
+    line = iota((QUAD, piece), 0)
+    corner = jnp.zeros((QUAD, piece), F32)
+    for p in range(pieces):
+        corner = jnp.where(line == 2 * p, cells[place : place + 1, p * piece : (p + 1) * piece], corner)
+    corner_ref[level] = corner.astype(BF16)
+
+
+def seed(entering, latents_ref, mask_ref, embed_ref, pieces, edges):
     levels, width = latents_ref.shape[2:]
     embed = embed_ref[...].astype(F32).reshape(1, width)
     across = WLON * levels
@@ -108,7 +132,9 @@
     at = iota((CELLS, CELLS * levels), 1)
     for level in range(levels):
         order = (at == wanted + level).astype(F32).astype(BF16)
-        store_quarters(dot(order, cells), entering, level, width, pieces)
+        ordered = dot(order, cells)
+        store_quarters(ordered, entering, level, width, pieces)
+        edges(ordered, level)
 
 
 def attended(q, k, v, bias, head_size):
@@ -151,10 +177,11 @@
 
 
 def kernel(
-    lat_signs, lon_signs,
-    offsets_ref, latents_ref, mask_ref, embed_ref, wqkv_hbm, wout_hbm, gain_ref, out_ref,
-    entering, leaving, wqkv, wout, main_in, tail_in, main_out, tail_out, bias, total,
-    weight_sem, send_sem, recv_sem, cross_send, cross_recv,
+    lat_signs, lon_signs, small_step,
+    offsets_hbm, latents_hbm, mask_hbm, embed_hbm, wqkv_hbm, wout_hbm, gain_hbm, out_ref,
+    offsets_ref, latents_ref, mask_ref, embed_ref, gain_ref,
+    entering, leaving, lines, corners, wqkv, wout, main_in, tail_in, main_out, tail_out, bias, total,
+    load_sem, send_sem, recv_sem, cross_send, cross_recv,
 ):
     segment, lon, lat = (lax.axis_index(axis) for axis in ("segment", "lon", "lat"))
     lons, lats = lax.axis_size("lon"), lax.axis_size("lat")
@@ -163,17 +190,61 @@
     at = lambda a, b: (segment, lax.rem(lon + b + lons, lons), lax.rem(lat + a + lats, lats))
     pick = lambda pair: pair[0] + segment * (pair[1] - pair[0])
 
-    loads = [
-        pltpu.make_async_copy(wqkv_hbm.at[0], wqkv, weight_sem.at[0]),
-        pltpu.make_async_copy(wout_hbm.at[0], wout, weight_sem.at[1]),
-    ]
-    for load in loads:
-        load.start()
     across = (1 - segment, lon, lat)
     partners = [at(a, b) for a in (-1, 0, 1) for b in (-1, 0, 1) if (a, b) != (0, 0)] + [across]
     barrier = pltpu.get_barrier_semaphore()
     for partner in partners:
         pl.semaphore_signal(barrier, inc=1, device_id=partner, device_id_type=pl.DeviceIdType.MESH)
+
+    def load(slot, source_ref, target_ref):
+        return pltpu.make_async_copy(source_ref, target_ref, load_sem.at[slot])
+
+    seeds = [load(0, latents_hbm, latents_ref), load(1, mask_hbm, mask_ref), load(2, embed_hbm, embed_ref)]
+    shifts, gains = load(3, offsets_hbm, offsets_ref), load(4, gain_hbm, gain_ref)
+    weights = [load(5, wqkv_hbm.at[0], wqkv), load(6, wout_hbm.at[0], wout)]
+
+    @pl.when(segment == 0)
+    def _():
+        for copy in seeds:
+            copy.start()
+
+    for copy in (shifts, gains, *weights):
+        copy.start()
+
+    on_small = segment == small_step
+    edge_lat, edge_lon = lat_signs[small_step][small_step], lon_signs[small_step][small_step]
+
+    def small_exchange(ref, level):
+        low, right = at(-edge_lat, 0), at(0, -edge_lon)
+        plan = (
+            (0, lines.at[level, pl.ds(0, QUAD)], (pl.ds(4 * QUAD, QUAD), pl.ds(0, width)), low),
+            (1, lines.at[level, pl.ds(QUAD, QUAD)], (pl.ds(6 * QUAD, QUAD), pl.ds(0, width)), right),
+            (3, corners.at[level], (pl.ds(8 * QUAD, QUAD), pl.ds(width, PAIR)), at(-edge_lat, -edge_lon)),
+        )
+        return [
+            pltpu.make_async_remote_copy(
+                src_ref=held,
+                dst_ref=ref.at[level, *target],
+                send_sem=send_sem.at[small_step, level, slot],
+                recv_sem=recv_sem.at[small_step, level, slot],
+                device_id=device,
+                device_id_type=pl.DeviceIdType.MESH,
+            )
+            for slot, held, target, device in plan
+        ]
+
+    def edges(cells, level):
+        store_edges(cells, edge_lat, edge_lon, lines, corners, level, pieces)
+
+    @pl.when(on_small)
+    def _():
+        ref = (entering, leaving)[small_step]
+        for level in range(levels):
+            for start in (5 * QUAD, 7 * QUAD):
+                ref[level, pl.ds(start, QUAD), :] = jnp.zeros((QUAD, width + PAIR), BF16)
+            for start in (4 * QUAD, 6 * QUAD):
+                ref[level, pl.ds(start, QUAD), pl.ds(width, PAIR)] = jnp.zeros((QUAD, PAIR), BF16)
+            ref[level, pl.ds(8 * QUAD, QUAD), pl.ds(0, width)] = jnp.zeros((QUAD, width), BF16)
 
     def exchange(index, ref, level):
         a, b = pick(lat_signs[index]), pick(lon_signs[index])
@@ -196,6 +267,23 @@
             for slot, (start, count, target, device) in enumerate(plan)
         ]
 
+    def each_transfer(index, level, act):
+        ref = (entering, leaving)[index]
+
+        def whole():
+            for copy in exchange(index, ref, level):
+                act(copy)
+
+        def edge():
+            for copy in small_exchange(ref, level):
+                act(copy)
+
+        if index == small_step:
+            pl.when(on_small)(edge)
+            pl.when(jnp.logical_not(on_small))(whole)
+        else:
+            whole()
+
     low_next = (1 - lat_signs[0][1]) // 2
 
     def crossing(level, part):
@@ -218,18 +306,23 @@
 
     @pl.when(segment == 0)
     def _():
-        seed(entering, latents_ref, mask_ref, embed_ref, pieces)
+        for copy in seeds:
+            copy.wait()
+        seed(
+            entering, latents_ref, mask_ref, embed_ref, pieces,
+            edges if small_step == 0 else lambda cells, level: None,
+        )
 
     pl.semaphore_wait(barrier, len(partners))
 
     def enter(level):
-        for copy in exchange(0, entering, level):
-            copy.start()
+        each_transfer(0, level, lambda copy: copy.start())
 
     @pl.when(segment == 0)
     def _():
         each_level(enter)
 
+    shifts.wait()
     lat_base = [based(offsets_ref[s, 0], WLAT) for s in (0, 1)]
     lon_base = [based(offsets_ref[s, 1], WLON) for s in (0, 1)]
     first = segment == 0
@@ -239,14 +332,17 @@
     offset = jnp.where(first, offsets_ref[0, 0], offsets_ref[1, 0])
 
     row, column = quarter_cell(iota((CELLS, 1), 0))
-    choosers(row + lat_in, column + lon_in, pick(lat_signs[0]), pick(lon_signs[0]), pieces, main_in, tail_in)
+    choosers(
+        row + lat_in, column + lon_in, pick(lat_signs[0]), pick(lon_signs[0]),
+        on_small if small_step == 0 else None, pieces, main_in, tail_in,
+    )
     line = iota((CELLS * levels, 1), 0)
     row, column = split_by(line, WLON * levels, WLAT)
     column, held_level = split_by(column, levels, WLON)
     for level in range(levels):
         choosers(
             row - lat_own, column - lon_own, pick(lat_signs[1]), pick(lon_signs[1]),
-            pieces, main_out.at[level], tail_out.at[level], held_level == level,
+            on_small if small_step == 1 else None, pieces, main_out.at[level], tail_out.at[level], held_level == level,
         )
 
     def wrapped(shape, axis):
@@ -259,8 +355,9 @@
     excluded = jnp.where(wrapped((CELLS, 1), 0) == wrapped((1, CELLS), 1), 0.0, -1e30)
     bias[pl.ds(0, CELLS), :] = excluded
     bias[pl.ds(CELLS, CELLS), :] = excluded
-    for load in loads:
-        load.wait()
+    gains.wait()
+    for copy in weights:
+        copy.wait()
 
     @pl.when(segment == 1)
     def _():
@@ -277,35 +374,34 @@
     gain = jnp.where(first, gain_ref[0:1, :], gain_ref[1:2, :])
 
     def work(level):
-        for copy in exchange(0, entering, level):
-            copy.wait_recv()
+        each_transfer(0, level, lambda copy: copy.wait_recv())
         x = gathered(entering[level], main_in, tail_in, width, pieces).astype(BF16)
-        store_quarters(section(x, bias[...], wqkv, wout, gain), leaving, level, width, pieces)
+        cells = section(x, bias[...], wqkv, wout, gain)
+        store_quarters(cells, leaving, level, width, pieces)
 
         @pl.when(segment == 0)
         def _():
             for part in (0, 1):
                 crossing(level, part).start()
 
-        for copy in exchange(1, leaving, level):
-            copy.start()
+        if small_step == 1:
+            pl.when(on_small)(lambda: edges(cells, level))
+        each_transfer(1, level, lambda copy: copy.start())
 
     each_level(work)
 
     total[...] = jnp.zeros_like(total)
 
     def finish(level):
-        for copy in exchange(1, leaving, level):
-            copy.wait_recv()
+        each_transfer(1, level, lambda copy: copy.wait_recv())
         total[...] += gathered(leaving[level], main_out.at[level], tail_out.at[level], width, pieces)
 
     each_level(finish)
     out_ref[...] = total[...].astype(BF16).reshape(out_ref.shape)
 
     def settle(level):
-        for index, ref in enumerate((entering, leaving)):
-            for copy in exchange(index, ref, level):
-                copy.wait_send()
+        for index in (0, 1):
+            each_transfer(index, level, lambda copy: copy.wait_send())
 
         @pl.when(segment == 0)
         def _():
@@ -331,13 +427,20 @@
     in_hbm = pl.BlockSpec(memory_space=pl.ANY)
     block = (levels, 9 * QUAD, width + PAIR)
     return pl.pallas_call(
-        functools.partial(kernel, signs[0], signs[1]),
+        functools.partial(kernel, signs[0], signs[1], int(second_known)),
         out_shape=jax.ShapeDtypeStruct(latents.shape, BF16),
-        in_specs=[pl.BlockSpec(memory_space=pltpu.SMEM), in_vmem, in_vmem, in_vmem, in_hbm, in_hbm, in_vmem],
+        in_specs=[in_hbm] * 7,
         out_specs=in_vmem,
         scratch_shapes=[
+            pltpu.SMEM(offsets.shape, offsets.dtype),
+            pltpu.VMEM(latents.shape, latents.dtype),
+            pltpu.VMEM(land_mask.shape, land_mask.dtype),
+            pltpu.VMEM(land_embed.shape, land_embed.dtype),
+            pltpu.VMEM(norm_gain.shape, norm_gain.dtype),
             pltpu.VMEM(block, BF16),
             pltpu.VMEM(block, BF16),
+            pltpu.VMEM((levels, 2 * QUAD, width), BF16),
+            pltpu.VMEM((levels, QUAD, PAIR), BF16),
             pltpu.VMEM(qkv_weight.shape[1:], BF16),
             pltpu.VMEM(out_weight.shape[1:], BF16),
             pltpu.VMEM((CELLS, 9 * QUAD), BF16),
@@ -346,7 +449,7 @@
             pltpu.VMEM((levels, CELLS * levels * pieces, 9 * QUAD), BF16),
             pltpu.VMEM((2 * CELLS, CELLS), F32),
             pltpu.VMEM((CELLS * levels, width), F32),
-            pltpu.SemaphoreType.DMA((2,)),
+            pltpu.SemaphoreType.DMA((7,)),
             pltpu.SemaphoreType.DMA((2, levels, 4)),
             pltpu.SemaphoreType.DMA((2, levels, 4)),
             pltpu.SemaphoreType.DMA((levels, 2)),

time: 34.5 us -> 33.4 us (0.968)
  Pallas kernels: 31 us -> 29.9 us
    pallas_call x1, Pallas kernels: 31 us -> 29.9 us  [sections(): pl.pallas_call(functools.partial(kernel, signs[0], signs[1], int(second_k...]
where the time goes in v3:
time: 33.4 us; the launch traced here: 33 us
  Pallas kernels  29.9 us (90%)
  other arithmetic  1.46 us (4%)
  local copies, waits for them, and re-layouts  0.72 us (2%)
  between operations  0.66 us (2%)
    pallas_call x1, Pallas kernels, sections(): pl.pallas_call(functools.partial(kernel, signs[0], signs[1], int(second_k...  29.9 us
    reduce_sum x1, other arithmetic, body(): variant = jnp.sum(term)  1.46 us
    unnamed x1, local copies, waits for them, and re-layouts  0.72 us

profile of v3, /device:TPU:5, one launch (start us, length us, event | category | flops | bytes accessed | tf_op | source)
XLA Modules:
  0.0 33.0 jit_solution(10050719094770419301)
XLA Ops:
  0.0 1.5 %fusion = s32[]{:T(128)} fusion(s32[2,2]{1,0:T(2,128)} %param.21), kind=kLoop, calls=%fused_computation.4 | loop fusion | flops 25 | bytes 20 | tf_op jit(solution)/shard_map/reduce_sum | solution.py:470
  2.1 30.1 %conditional.1 = (bf16[6,12,2,1024]{3,2,1,0:T(2,128)(2,1)S(1)}) conditional(s32[]{:T(128)} %clamp.3, (s32[2,2]{1,0:T(2,128)}, bf16[6,12,2,1024]{3,2,1,0:T(2,128)(2,1)}, s32[6,12]{1,0:T(8,128)}, bf16[1024]{0:T(1024)(128)(2,1)}, bf16[1,1024,3072]{2,1,0:T(8,128)(2,1)}, /*index=5*/bf16[1,1024,1024]{2,1,0:T(8,128)(2,1)}, ...), branch_computations={%region_1.2_spmd, %region_2.3_spmd, %region_3.4_spmd, %region_4.5_... | conditional | bytes 8 | solution.py:472
  2.4 29.9 %branch_5_fun.1 = bf16[6,12,2,1024]{3,2,1,0:T(2,128)(2,1)S(1)} custom-call(s32[2,2]{1,0:T(2,128)} %get-tuple-element.161.offsets_hbm, bf16[6,12,2,1024]{3,2,1,0:T(2,128)(2,1)} %get-tuple-element.162.latents_hbm, s32[6,12]{1,0:T(8,128)} %get-tuple-element.163.mask_hbm, bf16[1024]{0:T(1024)(128)(2,1)} %get-tuple-element.164.embed_hbm, ...), custom_call_target="tpu_custom_call" | custom-call | tf_op jit(solution)/shard_map/cond/branch_5_fun/pallas_call | solution.py:429
  32.3 0.7 %copy.17 = bf16[1,2,6,12,1024]{4,1,3,2,0:T(2,128)(2,1)} copy(bf16[1,2,6,12,1024]{4,1,3,2,0:T(2,128)(2,1)S(1)} %bitcast.12) | data formatting | bytes 589824
